TPU v7x, 32 devices: a whole 2x2x4 slice. The times are simulated.
32 devices in a mesh: src: 16 (over z, y, core), blk: 2 (over x).
Axes of the slice: x: 2, y: 2, z: 4, core: 2. Of those that a mesh axis runs over, the one named last changes fastest.
Arguments:
- source_points: bfloat16 [65536, 256], P(('src', 'blk')), may hold values from -40 to 40
- source_slot: int32 [32, 2048], P(('src', 'blk')), may hold values from 0 to 2047, each once within a row
- source_logw: float32 [65536], P(('src', 'blk')), may hold values from -2 to 2
- target_points: bfloat16 [2048, 256], P(('blk', 'src')), may hold values from -40 to 40
- target_logw: float32 [2048], P(('blk', 'src')), may hold values from -2 to 2
- target_pot: bfloat16 [2048], P(('blk', 'src')), may hold values from -6 to 6
- pair_mask: int32 [128, 4], P(('src', 'blk')), may hold values from 0 to 1, as said below
Outputs:
- source_pot: float32 [65536], P(('src', 'blk'))
- target_next: float32 [2048], P(('blk', 'src'))
Inputs may be any that keep to these rules, and one draw needn't show every extreme that they name: `pair_mask`: each source block p lists target block (p // 4) mod 4, so every source block and every target block has a listed pair. `source_slot`: each row is a permutation of 0 to 2047.
All inputs are finite; a program needn't handle non-finite values.
Results may differ from a plain program's by a relative error of at most 0.00035.
Values may be sent and summed in bfloat16 or wider, within the bound.
A program may use at most 64 MiB of HBM per device.

v0:
```python
import math
import functools

import jax
import jax.numpy as jnp
from jax import lax
from jax.experimental import pallas as pl
from jax.experimental.pallas import tpu as pltpu
from jax.sharding import PartitionSpec as P

BLOCK = 512
LANES = 128
CHUNK = 256
EPS = 0.25
FLOOR = -1e30
LOG2E = math.log2(math.e)
LN2 = math.log(2.0)


def dot_t(a, b):
    return lax.dot_general(a, b, (((1,), (1,)), ((), ())), preferred_element_type=jnp.float32)


def norm_row(points):
    wide = points.astype(jnp.float32)
    square = wide * wide
    high = square.astype(jnp.bfloat16)
    low = (square - high.astype(jnp.float32)).astype(jnp.bfloat16)
    ones = jnp.ones((8, points.shape[1]), jnp.bfloat16)
    return (dot_t(ones, high) + dot_t(ones, low))[0:1]


def column_of(row):
    return jnp.broadcast_to(row, (LANES, LANES)).T


def prepare_mask(slot_ref, pm_ref, mask_ref, ntb):
    pts = slot_ref.shape[1]
    nrow = pts // LANES
    nsb = pts // BLOCK
    slot = slot_ref[...]
    hits, highs = [], []
    for p in range(nsb):
        part = slot[:, p * BLOCK : (p + 1) * BLOCK]
        low = jnp.broadcast_to(part & (LANES - 1), (LANES, BLOCK))
        lane = lax.broadcasted_iota(jnp.int32, (LANES, BLOCK), 0)
        hits.append(jnp.where(low == lane, 1.0, 0.0).astype(jnp.bfloat16))
        high = jnp.broadcast_to(part >> 7, (nrow, BLOCK))
        highs.append(high == lax.broadcasted_iota(jnp.int32, (nrow, BLOCK), 0))
    for q in range(ntb):
        listed = jnp.zeros((nrow, LANES), jnp.float32)
        for p in range(nsb):
            value = pm_ref[p, q].astype(jnp.float32)
            picked = jnp.where(highs[p], value, 0.0).astype(jnp.bfloat16)
            listed = listed + dot_t(picked, hits[p])
        bias = jnp.where(listed > 0.5, 0.0, FLOOR)
        for a in range(nrow):
            mask_ref[q * nrow + a] = bias[a : a + 1]


def wide_row(ref, index):
    return jnp.concatenate([ref[index], ref[index + 1]], axis=1)


def row_pass(x_ref, t_ref, u_ref, mask_ref, logw_ref, pot_ref, g_ref, ntb):
    scale = LOG2E / 32.0
    nrow = x_ref.shape[0] // LANES
    group = min(ntb, 4)

    def one_chunk(ch, _):
        src = x_ref[pl.ds(pl.multiple_of(ch * CHUNK, CHUNK), CHUNK), :]

        def one_group(grp, state):
            peak, total = state
            for k in range(group):
                q = grp * group + k
                rows = pl.ds(pl.multiple_of(q * BLOCK, BLOCK), BLOCK)
                u = u_ref[rows, :]
                s = dot_t(t_ref[rows, :], src) + jnp.concatenate([u, u], axis=1)
                m = jnp.max(s, axis=0, keepdims=True)
                part = jnp.sum(jnp.exp2((s - m) * scale), axis=0, keepdims=True)
                m = m * scale + wide_row(mask_ref, q * nrow + 2 * ch)
                new = jnp.maximum(peak, m)
                total = total * jnp.exp2(peak - new) + part * jnp.exp2(m - new)
                peak = new
            return peak, total

        start = (jnp.full((1, CHUNK), FLOOR, jnp.float32), jnp.zeros((1, CHUNK), jnp.float32))
        if ntb == group:
            peak, total = one_group(0, start)
        else:
            peak, total = lax.fori_loop(0, ntb // group, one_group, start)
        lse = peak + jnp.log2(total)
        logw = wide_row(logw_ref, 2 * ch)
        g = (logw * LOG2E - lse) * (1.0 / scale)
        pot = EPS * (logw - lse * LN2 + norm_row(src) * (1.0 / 64.0))
        for h in range(2):
            cut = slice(h * LANES, (h + 1) * LANES)
            pot_ref[2 * ch + h] = pot[:, cut]
            g_ref[2 * ch + h] = g[:, cut]
        return 0

    lax.fori_loop(0, nrow // 2, one_chunk, 0)


def col_pass(x_ref, t_ref, mask_ref, g_ref, gcol_ref, out_ref, ntb):
    scale = LOG2E / 32.0
    pts = x_ref.shape[0]
    nrow = pts // LANES

    def one_block(q, _):
        for a in range(nrow):
            gcol_ref[a * LANES : (a + 1) * LANES, :] = column_of(g_ref[a] + mask_ref[q * nrow + a])

        def one_chunk(half, _):
            ch = q * (BLOCK // CHUNK) + half
            tgt = t_ref[pl.ds(pl.multiple_of(ch * CHUNK, CHUNK), CHUNK), :]
            peaks, totals = [], []
            for p in range(pts // BLOCK):
                g = gcol_ref[p * BLOCK : (p + 1) * BLOCK, :]
                s = dot_t(x_ref[p * BLOCK : (p + 1) * BLOCK, :], tgt) + jnp.concatenate([g, g], axis=1)
                m = jnp.max(s, axis=0, keepdims=True)
                totals.append(jnp.sum(jnp.exp2((s - m) * scale), axis=0, keepdims=True))
                peaks.append(m * scale)
            peak = functools.reduce(jnp.maximum, peaks)
            total = sum(l * jnp.exp2(m - peak) for m, l in zip(peaks, totals))
            lse = peak + jnp.log2(total)
            out_ref[2 * ch] = lse[:, :LANES]
            out_ref[2 * ch + 1] = lse[:, LANES:]
            return 0

        lax.fori_loop(0, BLOCK // CHUNK, one_chunk, 0)
        return 0

    lax.fori_loop(0, ntb, one_block, 0)


def compute_kernel(ntb, x_ref, slot_ref, logw_ref, t_ref, u_ref, pm_ref, pot_ref, out_ref, mask_ref, g_ref, ucol_ref, gcol_ref):
    prepare_mask(slot_ref, pm_ref, mask_ref, ntb)
    for a in range(u_ref.shape[0]):
        ucol_ref[a * LANES : (a + 1) * LANES, :] = column_of(u_ref[a])
    row_pass(x_ref, t_ref, ucol_ref, mask_ref, logw_ref, pot_ref, g_ref, ntb)
    col_pass(x_ref, t_ref, mask_ref, g_ref, gcol_ref, out_ref, ntb)


def body(source_points, source_slot, source_logw, target_points, target_logw, target_pot, pair_mask):
    axes = ("blk", "src")
    ndev = lax.axis_size("blk") * lax.axis_size("src")
    pts, dim = source_points.shape
    shard = target_points.shape[0]
    nt = shard * ndev
    ntb = nt // BLOCK
    nrow = pts // LANES
    wide = target_points.astype(jnp.float32)
    tnorm = jnp.sum(wide * wide, axis=1)
    u = target_pot.astype(jnp.float32) * 128.0 - 0.5 * tnorm
    t_all = lax.all_gather(target_points, axes, axis=0, tiled=True)
    u_all = lax.all_gather(u, axes, axis=0, tiled=True)
    vmem = pl.BlockSpec(memory_space=pltpu.VMEM)
    pot, lse = pl.pallas_call(
        functools.partial(compute_kernel, ntb),
        out_shape=(
            jax.ShapeDtypeStruct((nrow, 1, LANES), jnp.float32),
            jax.ShapeDtypeStruct((nt // LANES, 1, LANES), jnp.float32),
        ),
        in_specs=[vmem] * 5 + [pl.BlockSpec(memory_space=pltpu.SMEM)],
        out_specs=(vmem, vmem),
        scratch_shapes=[
            pltpu.VMEM((ntb * nrow, 1, LANES), jnp.float32),
            pltpu.VMEM((nrow, 1, LANES), jnp.float32),
            pltpu.VMEM((nt, LANES), jnp.float32),
            pltpu.VMEM((pts, LANES), jnp.float32),
        ],
        compiler_params=pltpu.CompilerParams(vmem_limit_bytes=48 * 1024 * 1024),
    )(
        source_points,
        source_slot,
        source_logw.reshape(nrow, 1, LANES),
        t_all,
        u_all.reshape(nt // LANES, 1, LANES),
        pair_mask,
    )
    parts = lax.all_to_all(lse.reshape(ndev, shard), axes, 0, 0, tiled=True)
    peak = jnp.max(parts, axis=0)
    total = jnp.sum(jnp.exp2(parts - peak), axis=0)
    col = (peak + jnp.log2(total)) * LN2 - tnorm * (1.0 / 64.0)
    return pot.reshape(pts), EPS * target_logw - EPS * col


def solution(mesh):
    in_specs = (
        P(("src", "blk"), None),
        P(("src", "blk"), None),
        P(("src", "blk")),
        P(("blk", "src"), None),
        P(("blk", "src")),
        P(("blk", "src")),
        P(("src", "blk"), None),
    )
    out_specs = (P(("src", "blk")), P(("blk", "src")))
    return jax.shard_map(body, mesh=mesh, in_specs=in_specs, out_specs=out_specs, check_vma=False)
```

profile of v0, /device:TPU:0, one launch (start us, length us, event | category | flops | bytes accessed | tf_op | source)
XLA Modules:
  0.0 106.1 jit_solution(5544762620536698524)
XLA Ops:
  7.2 0.0 copy-start.5
  7.2 0.0 all-gather.2.cloned.1.call-start
  7.2 0.7 all-gather.2.cloned.1.call-update
  7.9 0.0 copy-start.8
  7.9 0.6 copy-done.8
  8.6 0.6 dynamic-slice
  9.8 0.0 copy-done.5
  9.8 0.1 multiply_reduce_fusion
  9.9 0.0 copy-start.7
  9.9 0.6 copy-done.7
  10.6 0.1 subtract_dynamic-update-slice_fusion
  10.7 0.0 copy-start.2
  10.7 0.0 copy-start.3
  10.7 42.1 %all-reduce = f32[2048]{0:T(1024)S(1)} all-reduce(f32[2048]{0:T(1024)S(1)} %subtract_dynamic-update-slice_fusion), channel_id=1, replica_groups=mesh['src'=16,'blk'=2] {'blk','src'}, use_global_device_ids=true, to_apply=%add | all-reduce | flops 2048 | bytes 16384
  52.8 0.0 copy-start.4
  52.8 14.6 %all-gather.2.cloned.1.call-done.t_ref = bf16[2048,256]{1,0:T(8,128)(2,1)} async-done(((bf16[64,256]{1,0:T(8,128)(2,1)}), bf16[2048,256]{1,0:T(8,128)(2,1)}) %all-gather.2.cloned.1.call-update) | async-done | bytes 1048592 | tf_op jit(solution)/shard_map/all_gather | solution.py:157
  67.3 0.0 copy-done.2
  67.4 0.0 copy-done.3
  67.4 0.0 copy-done.4
  67.4 0.0 copy-start
  67.4 1.2 %copy-done = bf16[2048,256]{1,0:T(8,128)(2,1)S(1)} copy-done((bf16[2048,256]{1,0:T(8,128)(2,1)S(1)}, bf16[2048,256]{1,0:T(8,128)(2,1)}, u32[]{:S(2)}) %copy-start) | copy-done | bytes 1048600
  68.6 0.0 copy-start.1
  68.6 1.2 %copy-done.1 = bf16[2048,256]{1,0:T(8,128)(2,1)S(1)} copy-done((bf16[2048,256]{1,0:T(8,128)(2,1)S(1)}, bf16[2048,256]{1,0:T(8,128)(2,1)}, u32[]{:S(2)}) %copy-start.1) | copy-done | bytes 1048600
  69.8 16.5 %shard_map.86 = (f32[16,1,128]{2,1,0:T(1,128)}, f32[16,1,128]{2,1,0:T(1,128)S(1)}) custom-call(bf16[2048,256]{1,0:T(8,128)(2,1)S(1)} %copy-done, s32[1,2048]{1,0:T(1,128)S(1)} %copy-done.2, f32[16,1,128]{2,1,0:T(1,128)S(1)} %bitcast.7, bf16[2048,256]{1,0:T(8,128)(2,1)S(1)} %copy-done.1, f32[16,1,128]{2,1,0:T(1,128)S(1)} %bitcast.6, s32[4,4]{1,0:T(4,128)S(1)} %copy-done.4), custom_call_target="tpu_custom_call" | custom-call | tf_op jit(solution)/shard_map/pallas_call | solution.py:160
  86.3 0.5 broadcast.10
  86.8 0.7 reduce.4
  87.5 0.1 all_to_all.8
  87.6 10.5 %all_to_all.12 = f32[32,1,64]{2,1,0:T(1,128)S(1)} all-to-all(f32[32,1,64]{2,1,0:T(1,128)S(1)} %bitcast.9), channel_id=1, replica_groups=mesh['src'=16,'blk'=2] {'blk','src'}, dimensions={0} | all-to-all | bytes 16384 | tf_op jit(solution)/shard_map/all_to_all | solution.py:183
  98.1 0.1 reduce_max.9
  98.1 0.0 copy-start.6
  98.1 0.6 copy-done.6
  98.8 0.5 multiply_subtract_fusion
  (2 shorter events, 0.0 us)
Async XLA Ops:
  7.2 2.6 %copy-start.5 = (bf16[64,256]{1,0:T(8,128)(2,1)S(1)}, bf16[64,256]{1,0:T(8,128)(2,1)}, u32[]{:S(2)}) copy-start(bf16[64,256]{1,0:T(8,128)(2,1)} %param.10) | copy-start | bytes 98308
  7.2 60.2 %all-gather.2.cloned.1.call-start = ((), (), s32[]{:S(2)}) async-start(), calls=%async_computation.1 | async-start | bytes 1081344 | tf_op jit(solution)/shard_map/all_gather | solution.py:157
  7.9 0.7 copy-start.8
  9.9 0.7 copy-start.7
  10.7 56.7 %copy-start.2 = (s32[1,2048]{1,0:T(1,128)S(1)}, s32[1,2048]{1,0:T(1,128)}, u32[]{:S(2)}) copy-start(s32[1,2048]{1,0:T(1,128)} %slot_ref.1) | copy-start | bytes 24580
  10.7 56.7 %copy-start.3 = (f32[2048]{0:T(1024)S(1)}, f32[2048]{0:T(1024)}, u32[]{:S(2)}) copy-start(f32[2048]{0:T(1024)} %param.9) | copy-start | bytes 24580
  52.8 14.6 %copy-start.4 = (s32[4,4]{1,0:T(4,128)S(1)}, s32[4,4]{1,0:T(4,128)}, u32[]{:S(2)}) copy-start(s32[4,4]{1,0:T(4,128)} %pm_ref.1) | copy-start | bytes 196
  67.4 1.2 %copy-start = (bf16[2048,256]{1,0:T(8,128)(2,1)S(1)}, bf16[2048,256]{1,0:T(8,128)(2,1)}, u32[]{:S(2)}) copy-start(bf16[2048,256]{1,0:T(8,128)(2,1)} %x_ref.1) | copy-start | bytes 3145732
  68.6 1.2 %copy-start.1 = (bf16[2048,256]{1,0:T(8,128)(2,1)S(1)}, bf16[2048,256]{1,0:T(8,128)(2,1)}, u32[]{:S(2)}) copy-start(bf16[2048,256]{1,0:T(8,128)(2,1)} %all-gather.2.cloned.1.call-done.t_ref) | copy-start | bytes 3145732
  98.1 0.7 copy-start.6
Sparse Core Ops, SparseCore 0:
  10.9 56.4 all-gather.1
where the time goes:
time: 106 us
  blocking collectives  52.6 us (50%)
  Pallas kernels  16.5 us (16%)
  waiting for transfers between devices  15.3 us (14%)
  between operations  14.7 us (14%)
  local copies, waits for them, and re-layouts  5.55 us (5%)
  other arithmetic  1.47 us (1%)
    unnamed x1, blocking collectives  42.1 us
    pallas_call x1, Pallas kernels, body(): pl.pallas_call(functools.partial(compute_kernel, ntb), out_shape=(jax.Sha...  16.5 us
    all_gather x1, waiting for transfers between devices, body(): t_all = lax.all_gather(target_points, axes, axis=0, tiled=True)  14.6 us
    all_to_all x1, blocking collectives, body(): parts = lax.all_to_all(lse.reshape(ndev, shard), axes, 0, 0, tiled=True)  10.5 us
    unnamed x20, local copies, waits for them, and re-layouts  4.97 us
  transfers between devices with their start and end apart: 1, of which 1 were waited for; matrix products, arithmetic and copies ran while one was open for 1% of the time, Pallas kernels for 0%

commit v1 on v0

--- a/solution.py
+++ b/solution.py
@@ -135,56 +135,242 @@
     lax.fori_loop(0, ntb, one_block, 0)
 
 
-def compute_kernel(ntb, x_ref, slot_ref, logw_ref, t_ref, u_ref, pm_ref, pot_ref, out_ref, mask_ref, g_ref, ucol_ref, gcol_ref):
+def fused_kernel(
+    ntb, nsrc, nblk, x_hbm, slot_hbm, logw_hbm, tp_hbm, tpot_ref, tlogw_ref, pm_ref, pot_ref, next_ref,
+    x_ref, slot_ref, logw_ref, t_ref, mask_ref, g_ref, ucol_ref, gcol_ref, u_ref, lse_ref, rec_ref,
+    local_sem, pts_send, pts_recv, u_send, u_recv, lse_send, lse_recv,
+):
+    ndev = nsrc * nblk
+    nz = nsrc // 4
+    shard = tpot_ref.shape[1]
+    per = LANES // shard
+    s = lax.axis_index("src")
+    b = lax.axis_index("blk")
+    me = b * nsrc + s
+    z, y, c = s // 4, s // 2 % 2, s % 2
+
+    def rows_of(t):
+        return t_ref.at[pl.ds(pl.multiple_of(t * shard, shard), shard), :]
+
+    loads = [
+        pltpu.make_async_copy(tp_hbm, rows_of(me), local_sem.at[0]),
+        pltpu.make_async_copy(slot_hbm, slot_ref, local_sem.at[1]),
+        pltpu.make_async_copy(logw_hbm, logw_ref, local_sem.at[2]),
+        pltpu.make_async_copy(x_hbm, x_ref, local_sem.at[3]),
+    ]
+    for load in loads:
+        load.start()
+
+    barrier = pltpu.get_barrier_semaphore()
+
+    def target(k):
+        t = (me + k) % ndev
+        return t, (t % nsrc, t // nsrc)
+
+    def greet(k, _):
+        pl.semaphore_signal(barrier, inc=1, device_id=target(k)[1], device_id_type=pl.DeviceIdType.MESH)
+        return 0
+
+    lax.fori_loop(1, ndev, greet, 0)
+
+    loads[0].wait()
+    tnorm = norm_row(rows_of(me)[...])
+    u = tpot_ref[...].astype(jnp.float32) * 128.0 - 0.5 * tnorm
+    if shard < LANES:
+        u = jnp.concatenate([u, jnp.zeros((1, LANES - shard), jnp.float32)], axis=1)
+    u_ref[me] = u
+    loads[1].wait()
     prepare_mask(slot_ref, pm_ref, mask_ref, ntb)
-    for a in range(u_ref.shape[0]):
-        ucol_ref[a * LANES : (a + 1) * LANES, :] = column_of(u_ref[a])
+
+    pl.semaphore_wait(barrier, ndev - 1)
+
+    def send(t, dev_s, dev_b):
+        pltpu.make_async_remote_copy(
+            src_ref=rows_of(t), dst_ref=rows_of(t), send_sem=pts_send, recv_sem=pts_recv.at[t],
+            device_id=(dev_s, dev_b), device_id_type=pl.DeviceIdType.MESH,
+        ).start()
+
+    def arrived(t):
+        pltpu.make_async_copy(rows_of(t), rows_of(t), pts_recv.at[t]).wait()
+
+    def slot_of(bb, zz, yy):
+        return bb * nsrc + zz * 4 + yy * 2 + c
+
+    def to_y(t):
+        send(t, z * 4 + (1 - y) * 2 + c, b)
+
+    def to_blk(t):
+        for k in range(1, nblk):
+            send(t, s, (b + k) % nblk)
+
+    def to_core(t):
+        send(t, z * 4 + y * 2 + (1 - c), b)
+
+    for k in range(1, nz):
+        send(me, (z + k) % nz * 4 + y * 2 + c, b)
+
+    def send_u(k, _):
+        pltpu.make_async_remote_copy(
+            src_ref=u_ref.at[me], dst_ref=u_ref.at[me], send_sem=u_send, recv_sem=u_recv,
+            device_id=target(k)[1], device_id_type=pl.DeviceIdType.MESH,
+        ).start()
+        return 0
+
+    def plane(k, first):
+        t = slot_of(b, (z + k) % nz, y)
+        if not first:
+            arrived(t)
+        to_y(t)
+        to_blk(t)
+        to_core(t)
+        return 0
+
+    plane(0, True)
+    lax.fori_loop(1, ndev, send_u, 0)
+    lax.fori_loop(1, nz, lambda k, _: plane(k, False), 0)
+
+    def pass_on(bb, zz, yy, onward):
+        t = slot_of(bb, zz, yy)
+        arrived(t)
+        if onward is not None:
+            onward(t)
+        to_core(t)
+
+    def drain(count):
+        def one(_, carry):
+            pltpu.make_async_copy(rows_of(me), rows_of(me), pts_send).wait()
+            return carry
+
+        lax.fori_loop(0, count, one, 0)
+
+    @pl.when(c == 0)
+    def _():
+        def near(k, _):
+            pass_on(b, (z + k) % nz, 1 - y, to_blk)
+            return 0
+
+        lax.fori_loop(0, nz, near, 0)
+
+        def far(k, _):
+            bb = (b + 1 + k // nz) % nblk
+            pass_on(bb, (z + k) % nz, y, None)
+            pass_on(bb, (z + k) % nz, 1 - y, None)
+            return 0
+
+        lax.fori_loop(0, nz * (nblk - 1), far, 0)
+
+    @pl.when(c == 1)
+    def _():
+        def near(k, _):
+            pass_on((b + 1 + k // nz) % nblk, (z + k) % nz, y, to_y)
+            return 0
+
+        lax.fori_loop(0, nz * (nblk - 1), near, 0)
+
+        def far(k, _):
+            pass_on((b + k // nz) % nblk, (z + k) % nz, 1 - y, None)
+            return 0
+
+        lax.fori_loop(0, nz * nblk, far, 0)
+
+    others = u_ref.at[pl.ds(0, ndev - 1)]
+    pltpu.make_async_copy(others, others, u_recv).wait()
+    for t in range(ndev):
+        ucol_ref[t * shard : (t + 1) * shard, :] = column_of(u_ref[t])[:shard]
+
+    def other_core(k, _):
+        pltpu.make_async_copy(rows_of(me), rows_of(me), pts_recv.at[2 * k + 1 - c]).wait()
+        return 0
+
+    lax.fori_loop(0, ndev // 2, other_core, 0)
+    loads[2].wait()
+    loads[3].wait()
+
     row_pass(x_ref, t_ref, ucol_ref, mask_ref, logw_ref, pot_ref, g_ref, ntb)
-    col_pass(x_ref, t_ref, mask_ref, g_ref, gcol_ref, out_ref, ntb)
+    col_pass(x_ref, t_ref, mask_ref, g_ref, gcol_ref, lse_ref, ntb)
+
+    rec_ref[me] = lse_ref[me // per]
+
+    def send_lse(k, _):
+        t, where = target(k)
+        pltpu.make_async_remote_copy(
+            src_ref=lse_ref.at[t // per], dst_ref=rec_ref.at[me], send_sem=lse_send, recv_sem=lse_recv,
+            device_id=where, device_id_type=pl.DeviceIdType.MESH,
+        ).start()
+        return 0
+
+    lax.fori_loop(1, ndev, send_lse, 0)
+    @pl.when(c == 0)
+    def _():
+        drain(nz - 1 + nz + 2 * nz * (nblk - 1) + 2 * nz * nblk)
+
+    @pl.when(c == 1)
+    def _():
+        drain(nz - 1 + nz * (nblk - 1) + nz * nblk + 2 * nz * nblk)
+
+    pltpu.make_async_copy(others, others, u_send).wait()
+    received = rec_ref.at[pl.ds(0, ndev - 1)]
+    pltpu.make_async_copy(received, received, lse_recv).wait()
+    pltpu.make_async_copy(received, received, lse_send).wait()
+    parts = rec_ref[...]
+    peak = jnp.max(parts, axis=0)
+    total = jnp.sum(jnp.exp2(parts - peak[None]), axis=0)
+    lse = peak + jnp.log2(total)
+    mine = lse[:, :shard]
+    for k in range(1, per):
+        mine = jnp.where(s % per == k, lse[:, k * shard : (k + 1) * shard], mine)
+    next_ref[...] = EPS * (tlogw_ref[...] - mine * LN2 + tnorm * (1.0 / 64.0))
 
 
 def body(source_points, source_slot, source_logw, target_points, target_logw, target_pot, pair_mask):
-    axes = ("blk", "src")
-    ndev = lax.axis_size("blk") * lax.axis_size("src")
+    nsrc, nblk = lax.axis_size("src"), lax.axis_size("blk")
+    ndev = nsrc * nblk
     pts, dim = source_points.shape
     shard = target_points.shape[0]
     nt = shard * ndev
     ntb = nt // BLOCK
     nrow = pts // LANES
-    wide = target_points.astype(jnp.float32)
-    tnorm = jnp.sum(wide * wide, axis=1)
-    u = target_pot.astype(jnp.float32) * 128.0 - 0.5 * tnorm
-    t_all = lax.all_gather(target_points, axes, axis=0, tiled=True)
-    u_all = lax.all_gather(u, axes, axis=0, tiled=True)
     vmem = pl.BlockSpec(memory_space=pltpu.VMEM)
-    pot, lse = pl.pallas_call(
-        functools.partial(compute_kernel, ntb),
-        out_shape=(
-            jax.ShapeDtypeStruct((nrow, 1, LANES), jnp.float32),
-            jax.ShapeDtypeStruct((nt // LANES, 1, LANES), jnp.float32),
-        ),
-        in_specs=[vmem] * 5 + [pl.BlockSpec(memory_space=pltpu.SMEM)],
+    hbm = pl.BlockSpec(memory_space=pl.ANY)
+    f32 = jnp.float32
+    pot, fresh = pl.pallas_call(
+        functools.partial(fused_kernel, ntb, nsrc, nblk),
+        out_shape=(jax.ShapeDtypeStruct((nrow, 1, LANES), f32), jax.ShapeDtypeStruct((1, shard), f32)),
+        in_specs=[hbm] * 4 + [vmem] * 2 + [pl.BlockSpec(memory_space=pltpu.SMEM)],
         out_specs=(vmem, vmem),
         scratch_shapes=[
-            pltpu.VMEM((ntb * nrow, 1, LANES), jnp.float32),
-            pltpu.VMEM((nrow, 1, LANES), jnp.float32),
-            pltpu.VMEM((nt, LANES), jnp.float32),
-            pltpu.VMEM((pts, LANES), jnp.float32),
+            pltpu.VMEM((pts, dim), jnp.bfloat16),
+            pltpu.VMEM((1, pts), jnp.int32),
+            pltpu.VMEM((nrow, 1, LANES), f32),
+            pltpu.VMEM((nt, dim), jnp.bfloat16),
+            pltpu.VMEM((ntb * nrow, 1, LANES), f32),
+            pltpu.VMEM((nrow, 1, LANES), f32),
+            pltpu.VMEM((nt, LANES), f32),
+            pltpu.VMEM((pts, LANES), f32),
+            pltpu.VMEM((ndev, 1, LANES), f32),
+            pltpu.VMEM((nt // LANES, 1, LANES), f32),
+            pltpu.VMEM((ndev, 1, LANES), f32),
+            pltpu.SemaphoreType.DMA((4,)),
+            pltpu.SemaphoreType.DMA,
+            pltpu.SemaphoreType.DMA((ndev,)),
+            pltpu.SemaphoreType.DMA,
+            pltpu.SemaphoreType.DMA,
+            pltpu.SemaphoreType.DMA,
+            pltpu.SemaphoreType.DMA,
         ],
-        compiler_params=pltpu.CompilerParams(vmem_limit_bytes=48 * 1024 * 1024),
+        compiler_params=pltpu.CompilerParams(
+            collective_id=0, has_side_effects=True, vmem_limit_bytes=48 * 1024 * 1024
+        ),
     )(
         source_points,
         source_slot,
         source_logw.reshape(nrow, 1, LANES),
-        t_all,
-        u_all.reshape(nt // LANES, 1, LANES),
+        target_points,
+        target_pot.reshape(1, shard),
+        target_logw.reshape(1, shard),
         pair_mask,
     )
-    parts = lax.all_to_all(lse.reshape(ndev, shard), axes, 0, 0, tiled=True)
-    peak = jnp.max(parts, axis=0)
-    total = jnp.sum(jnp.exp2(parts - peak), axis=0)
-    col = (peak + jnp.log2(total)) * LN2 - tnorm * (1.0 / 64.0)
-    return pot.reshape(pts), EPS * target_logw - EPS * col
+    return pot.reshape(pts), fresh.reshape(shard)
 
 
 def solution(mesh):

time: 106 us -> 46.5 us (0.44)
  blocking collectives: 52.6 us -> 0 us
  Pallas kernels: 16.5 us -> 40.4 us
  waiting for transfers between devices: 15.3 us -> 0 us
  between operations: 14.7 us -> 0.67 us
  other arithmetic: 1.47 us -> 0 us
    unnamed x1 -> x0, blocking collectives: 42.1 us -> none
    pallas_call x1, Pallas kernels: 16.5 us -> 40.4 us  [body(): pl.pallas_call(functools.partial(fused_kernel, ntb, nsrc, nblk), out_shap...]
    all_gather x1 -> x0, waiting for transfers between devices: 14.6 us -> none  [body(): t_all = lax.all_gather(target_points, axes, axis=0, tiled=True)]
    all_to_all x1 -> x0, blocking collectives: 10.5 us -> none  [body(): parts = lax.all_to_all(lse.reshape(ndev, shard), axes, 0, 0, tiled=True)]
    unnamed x20 -> x16, local copies, waits for them, and re-layouts: 4.97 us -> 5.15 us
  transfers between devices with their start and end apart: 1 -> 0, of which waited for: 1 -> 0; matrix products, arithmetic and copies ran while one was open for 1% -> 0% of each run, Pallas kernels for 0% -> 0%
where the time goes in v1:
time: 46.5 us; the launch traced here: 46.2 us
  Pallas kernels  40.4 us (87%)
  local copies, waits for them, and re-layouts  5.15 us (11%)
  between operations  0.67 us (1%)
    pallas_call x1, Pallas kernels, body(): pl.pallas_call(functools.partial(fused_kernel, ntb, nsrc, nblk), out_shap...  40.4 us
    unnamed x16, local copies, waits for them, and re-layouts  5.15 us

profile of v1, /device:TPU:0, one launch (start us, length us, event | category | flops | bytes accessed | tf_op | source)
XLA Modules:
  0.0 46.2 jit_solution(2363830425817644379)
XLA Ops:
  0.6 0.0 copy-start.4
  0.6 0.0 copy-start.5
  0.7 0.0 copy-start.6
  0.7 0.7 %copy-done.4 = s32[4,4]{1,0:T(4,128)S(1)} copy-done((s32[4,4]{1,0:T(4,128)S(1)}, s32[4,4]{1,0:T(4,128)}, u32[]{:S(2)}) %copy-start.4) | copy-done | bytes 88
  1.3 0.0 copy-done.5
  1.3 0.0 copy-done.6
  1.3 0.0 copy-start
  1.3 1.2 %copy-done = bf16[2048,256]{1,0:T(8,128)(2,1)S(1)} copy-done((bf16[2048,256]{1,0:T(8,128)(2,1)S(1)}, bf16[2048,256]{1,0:T(8,128)(2,1)}, u32[]{:S(2)}) %copy-start) | copy-done | bytes 1048600
  2.5 0.0 copy-start.1
  2.5 0.8 %copy-done.1 = bf16[64,256]{1,0:T(8,128)(2,1)S(1)} copy-done((bf16[64,256]{1,0:T(8,128)(2,1)S(1)}, bf16[64,256]{1,0:T(8,128)(2,1)}, u32[]{:S(2)}) %copy-start.1) | copy-done | bytes 32792
  3.3 0.0 copy-start.2
  3.3 0.7 %copy-done.2 = s32[1,2048]{1,0:T(1,128)S(1)} copy-done((s32[1,2048]{1,0:T(1,128)S(1)}, s32[1,2048]{1,0:T(1,128)}, u32[]{:S(2)}) %copy-start.2) | copy-done | bytes 8216
  4.0 0.0 copy-start.3
  4.0 0.7 %copy-done.3 = f32[2048]{0:T(1024)S(1)} copy-done((f32[2048]{0:T(1024)S(1)}, f32[2048]{0:T(1024)}, u32[]{:S(2)}) %copy-start.3) | copy-done | bytes 8216
  4.7 40.4 %shard_map.86 = (f32[16,1,128]{2,1,0:T(1,128)S(1)}, f32[1,64]{1,0:T(1,128)S(1)}) custom-call(bf16[2048,256]{1,0:T(8,128)(2,1)S(1)} %copy-done, s32[1,2048]{1,0:T(1,128)S(1)} %copy-done.2, f32[16,1,128]{2,1,0:T(1,128)S(1)} %bitcast.5, bf16[64,256]{1,0:T(8,128)(2,1)S(1)} %copy-done.1, bf16[1,64]{1,0:T(2,128)(2,1)S(1)} %bitcast.7, f32[1,64]{1,0:T(1,128)S(1)} %bitcast.8, ...), custom_call_target="tpu_custom_call" | custom-call | tf_op jit(solution)/shard_map/pallas_call | solution.py:336
  45.1 0.6 %copy.11 = f32[2048]{0:T(1024)} copy(f32[2048]{0:T(1024)S(1)} %bitcast.6) | data formatting | bytes 16384
  45.7 0.5 %copy.12 = f32[64]{0:T(128)} copy(f32[64]{0:T(128)S(1)} %bitcast.9) | data formatting | bytes 512
Async XLA Ops:
  0.6 0.7 %copy-start.4 = (s32[4,4]{1,0:T(4,128)S(1)}, s32[4,4]{1,0:T(4,128)}, u32[]{:S(2)}) copy-start(s32[4,4]{1,0:T(4,128)} %pm_ref.1) | copy-start | bytes 196
  0.6 0.7 %copy-start.5 = (bf16[64]{0:T(256)(128)(2,1)S(1)}, bf16[64]{0:T(256)(128)(2,1)}, u32[]{:S(2)}) copy-start(bf16[64]{0:T(256)(128)(2,1)} %param.12) | copy-start | bytes 388
  0.7 0.7 %copy-start.6 = (f32[64]{0:T(128)S(1)}, f32[64]{0:T(128)}, u32[]{:S(2)}) copy-start(f32[64]{0:T(128)} %param.11) | copy-start | bytes 772
  1.3 1.2 %copy-start = (bf16[2048,256]{1,0:T(8,128)(2,1)S(1)}, bf16[2048,256]{1,0:T(8,128)(2,1)}, u32[]{:S(2)}) copy-start(bf16[2048,256]{1,0:T(8,128)(2,1)} %x_hbm.1) | copy-start | bytes 3145732
  2.5 0.8 %copy-start.1 = (bf16[64,256]{1,0:T(8,128)(2,1)S(1)}, bf16[64,256]{1,0:T(8,128)(2,1)}, u32[]{:S(2)}) copy-start(bf16[64,256]{1,0:T(8,128)(2,1)} %tp_hbm.1) | copy-start | bytes 98308
  3.3 0.7 %copy-start.2 = (s32[1,2048]{1,0:T(1,128)S(1)}, s32[1,2048]{1,0:T(1,128)}, u32[]{:S(2)}) copy-start(s32[1,2048]{1,0:T(1,128)} %slot_hbm.1) | copy-start | bytes 24580
  4.0 0.7 %copy-start.3 = (f32[2048]{0:T(1024)S(1)}, f32[2048]{0:T(1024)}, u32[]{:S(2)}) copy-start(f32[2048]{0:T(1024)} %param.9) | copy-start | bytes 24580

commit v2 on v1

--- a/solution.py
+++ b/solution.py
@@ -62,10 +62,10 @@
     return jnp.concatenate([ref[index], ref[index + 1]], axis=1)
 
 
-def row_pass(x_ref, t_ref, u_ref, mask_ref, logw_ref, pot_ref, g_ref, ntb):
+def row_phase(x_ref, t_ref, u_ref, mask_ref, peak_ref, total_ref, base, count, ntb):
     scale = LOG2E / 32.0
     nrow = x_ref.shape[0] // LANES
-    group = min(ntb, 4)
+    group = min(count, 4)
 
     def one_chunk(ch, _):
         src = x_ref[pl.ds(pl.multiple_of(ch * CHUNK, CHUNK), CHUNK), :]
@@ -73,34 +73,38 @@
         def one_group(grp, state):
             peak, total = state
             for k in range(group):
-                q = grp * group + k
-                rows = pl.ds(pl.multiple_of(q * BLOCK, BLOCK), BLOCK)
+                piece = base + grp * group + k
+                rows = pl.ds(pl.multiple_of(piece * CHUNK, CHUNK), CHUNK)
                 u = u_ref[rows, :]
                 s = dot_t(t_ref[rows, :], src) + jnp.concatenate([u, u], axis=1)
                 m = jnp.max(s, axis=0, keepdims=True)
                 part = jnp.sum(jnp.exp2((s - m) * scale), axis=0, keepdims=True)
-                m = m * scale + wide_row(mask_ref, q * nrow + 2 * ch)
+                m = m * scale + wide_row(mask_ref, piece % ntb * nrow + 2 * ch)
                 new = jnp.maximum(peak, m)
                 total = total * jnp.exp2(peak - new) + part * jnp.exp2(m - new)
                 peak = new
             return peak, total
 
-        start = (jnp.full((1, CHUNK), FLOOR, jnp.float32), jnp.zeros((1, CHUNK), jnp.float32))
-        if ntb == group:
-            peak, total = one_group(0, start)
+        state = (wide_row(peak_ref, 2 * ch), wide_row(total_ref, 2 * ch))
+        if count == group:
+            peak, total = one_group(0, state)
         else:
-            peak, total = lax.fori_loop(0, ntb // group, one_group, start)
-        lse = peak + jnp.log2(total)
-        logw = wide_row(logw_ref, 2 * ch)
-        g = (logw * LOG2E - lse) * (1.0 / scale)
-        pot = EPS * (logw - lse * LN2 + norm_row(src) * (1.0 / 64.0))
+            peak, total = lax.fori_loop(0, count // group, one_group, state)
         for h in range(2):
             cut = slice(h * LANES, (h + 1) * LANES)
-            pot_ref[2 * ch + h] = pot[:, cut]
-            g_ref[2 * ch + h] = g[:, cut]
+            peak_ref[2 * ch + h] = peak[:, cut]
+            total_ref[2 * ch + h] = total[:, cut]
         return 0
 
     lax.fori_loop(0, nrow // 2, one_chunk, 0)
+
+
+def row_finish(norm_ref, logw_ref, peak_ref, total_ref, pot_ref, g_ref):
+    scale = LOG2E / 32.0
+    lse = peak_ref[...] + jnp.log2(total_ref[...])
+    logw = logw_ref[...]
+    g_ref[...] = (logw * LOG2E - lse) * (1.0 / scale)
+    pot_ref[...] = EPS * (logw - lse * LN2 + norm_ref[...] * (1.0 / 64.0))
 
 
 def col_pass(x_ref, t_ref, mask_ref, g_ref, gcol_ref, out_ref, ntb):
@@ -113,7 +117,7 @@
             gcol_ref[a * LANES : (a + 1) * LANES, :] = column_of(g_ref[a] + mask_ref[q * nrow + a])
 
         def one_chunk(half, _):
-            ch = q * (BLOCK // CHUNK) + half
+            ch = half * ntb + q
             tgt = t_ref[pl.ds(pl.multiple_of(ch * CHUNK, CHUNK), CHUNK), :]
             peaks, totals = [], []
             for p in range(pts // BLOCK):
@@ -135,19 +139,33 @@
     lax.fori_loop(0, ntb, one_block, 0)
 
 
+def merged(parts):
+    peak = jnp.max(parts, axis=0)
+    return peak + jnp.log2(jnp.sum(jnp.exp2(parts - peak[None]), axis=0))
+
+
 def fused_kernel(
     ntb, nsrc, nblk, x_hbm, slot_hbm, logw_hbm, tp_hbm, tpot_ref, tlogw_ref, pm_ref, pot_ref, next_ref,
     x_ref, slot_ref, logw_ref, t_ref, mask_ref, g_ref, ucol_ref, gcol_ref, u_ref, lse_ref, rec_ref,
+    mid_ref, last_ref, norm_ref, peak_ref, total_ref,
     local_sem, pts_send, pts_recv, u_send, u_recv, lse_send, lse_recv,
 ):
     ndev = nsrc * nblk
     nz = nsrc // 4
+    nplane = 4 * nblk
     shard = tpot_ref.shape[1]
     per = LANES // shard
+    keep = 2 * nz // per
+    per_group = ntb // nblk
     s = lax.axis_index("src")
     b = lax.axis_index("blk")
-    me = b * nsrc + s
     z, y, c = s // 4, s // 2 % 2, s % 2
+
+    def slot_at(cc, bb, zz, yy):
+        return ((cc * nblk + bb) * nz + zz) * 2 + yy
+
+    me = slot_at(c, b, z, y)
+    plane_me = (c * nblk + b) * 2 + y
 
     def rows_of(t):
         return t_ref.at[pl.ds(pl.multiple_of(t * shard, shard), shard), :]
@@ -162,39 +180,38 @@
         load.start()
 
     barrier = pltpu.get_barrier_semaphore()
-
-    def target(k):
-        t = (me + k) % ndev
-        return t, (t % nsrc, t // nsrc)
-
-    def greet(k, _):
-        pl.semaphore_signal(barrier, inc=1, device_id=target(k)[1], device_id_type=pl.DeviceIdType.MESH)
-        return 0
-
-    lax.fori_loop(1, ndev, greet, 0)
+    mesh_id = pl.DeviceIdType.MESH
+
+    def plane_peer(k):
+        p = (plane_me + k) % nplane
+        return p, (z * 4 + p % 2 * 2 + p // (2 * nblk), p // 2 % nblk)
+
+    def z_peer(k):
+        zz = (z + k) % nz
+        return zz, (zz * 4 + y * 2 + c, b)
+
+    for k in range(1, nz):
+        pl.semaphore_signal(barrier, inc=1, device_id=z_peer(k)[1], device_id_type=mesh_id)
+    for k in range(1, nplane):
+        pl.semaphore_signal(barrier, inc=1, device_id=plane_peer(k)[1], device_id_type=mesh_id)
 
     loads[0].wait()
     tnorm = norm_row(rows_of(me)[...])
     u = tpot_ref[...].astype(jnp.float32) * 128.0 - 0.5 * tnorm
     if shard < LANES:
         u = jnp.concatenate([u, jnp.zeros((1, LANES - shard), jnp.float32)], axis=1)
-    u_ref[me] = u
-    loads[1].wait()
-    prepare_mask(slot_ref, pm_ref, mask_ref, ntb)
-
-    pl.semaphore_wait(barrier, ndev - 1)
+    u_ref[plane_me * nz + z] = u
+
+    pl.semaphore_wait(barrier, nplane + nz - 2)
 
     def send(t, dev_s, dev_b):
         pltpu.make_async_remote_copy(
             src_ref=rows_of(t), dst_ref=rows_of(t), send_sem=pts_send, recv_sem=pts_recv.at[t],
-            device_id=(dev_s, dev_b), device_id_type=pl.DeviceIdType.MESH,
+            device_id=(dev_s, dev_b), device_id_type=mesh_id,
         ).start()
 
     def arrived(t):
         pltpu.make_async_copy(rows_of(t), rows_of(t), pts_recv.at[t]).wait()
-
-    def slot_of(bb, zz, yy):
-        return bb * nsrc + zz * 4 + yy * 2 + c
 
     def to_y(t):
         send(t, z * 4 + (1 - y) * 2 + c, b)
@@ -206,42 +223,56 @@
     def to_core(t):
         send(t, z * 4 + y * 2 + (1 - c), b)
 
+    def small(src, dst, send_sem, recv_sem, where):
+        pltpu.make_async_remote_copy(
+            src_ref=src, dst_ref=dst, send_sem=send_sem, recv_sem=recv_sem, device_id=where, device_id_type=mesh_id
+        ).start()
+
+    def rows_done(ref, count, sem):
+        part = ref.at[pl.ds(0, count)]
+        pltpu.make_async_copy(part, part, sem).wait()
+
     for k in range(1, nz):
-        send(me, (z + k) % nz * 4 + y * 2 + c, b)
-
-    def send_u(k, _):
-        pltpu.make_async_remote_copy(
-            src_ref=u_ref.at[me], dst_ref=u_ref.at[me], send_sem=u_send, recv_sem=u_recv,
-            device_id=target(k)[1], device_id_type=pl.DeviceIdType.MESH,
-        ).start()
-        return 0
-
-    def plane(k, first):
-        t = slot_of(b, (z + k) % nz, y)
-        if not first:
-            arrived(t)
+        send(me, *z_peer(k)[1])
+    for k in range(1, nz):
+        mine = u_ref.at[plane_me * nz + z]
+        small(mine, mine, u_send, u_recv.at[0], z_peer(k)[1])
+    to_y(me)
+    to_blk(me)
+    to_core(me)
+
+    loads[1].wait()
+    prepare_mask(slot_ref, pm_ref, mask_ref, ntb)
+
+    def plane(k, _):
+        t = slot_at(c, b, (z + k) % nz, y)
+        arrived(t)
         to_y(t)
         to_blk(t)
         to_core(t)
         return 0
 
-    plane(0, True)
-    lax.fori_loop(1, ndev, send_u, 0)
-    lax.fori_loop(1, nz, lambda k, _: plane(k, False), 0)
+    lax.fori_loop(1, nz, plane, 0)
+
+    rows_done(u_ref, nz - 1, u_recv.at[0])
+    for k in range(1, nplane):
+        group = u_ref.at[pl.ds(plane_me * nz, nz)]
+        small(group, group, u_send, u_recv.at[1], plane_peer(k)[1])
+
+    loads[3].wait()
+    for a in range(x_ref.shape[0] // CHUNK):
+        norm = norm_row(x_ref[a * CHUNK : (a + 1) * CHUNK, :])
+        norm_ref[2 * a] = norm[:, :LANES]
+        norm_ref[2 * a + 1] = norm[:, LANES:]
+    peak_ref[...] = jnp.full(peak_ref.shape, FLOOR, jnp.float32)
+    total_ref[...] = jnp.zeros(total_ref.shape, jnp.float32)
 
     def pass_on(bb, zz, yy, onward):
-        t = slot_of(bb, zz, yy)
+        t = slot_at(c, bb, zz, yy)
         arrived(t)
         if onward is not None:
             onward(t)
         to_core(t)
-
-    def drain(count):
-        def one(_, carry):
-            pltpu.make_async_copy(rows_of(me), rows_of(me), pts_send).wait()
-            return carry
-
-        lax.fori_loop(0, count, one, 0)
 
     @pl.when(c == 0)
     def _():
@@ -251,14 +282,6 @@
 
         lax.fori_loop(0, nz, near, 0)
 
-        def far(k, _):
-            bb = (b + 1 + k // nz) % nblk
-            pass_on(bb, (z + k) % nz, y, None)
-            pass_on(bb, (z + k) % nz, 1 - y, None)
-            return 0
-
-        lax.fori_loop(0, nz * (nblk - 1), far, 0)
-
     @pl.when(c == 1)
     def _():
         def near(k, _):
@@ -267,39 +290,67 @@
 
         lax.fori_loop(0, nz * (nblk - 1), near, 0)
 
-        def far(k, _):
-            pass_on((b + k // nz) % nblk, (z + k) % nz, 1 - y, None)
+        def home(k, _):
+            pass_on(b, (z + k) % nz, 1 - y, None)
             return 0
 
-        lax.fori_loop(0, nz * nblk, far, 0)
-
-    others = u_ref.at[pl.ds(0, ndev - 1)]
-    pltpu.make_async_copy(others, others, u_recv).wait()
-    for t in range(ndev):
-        ucol_ref[t * shard : (t + 1) * shard, :] = column_of(u_ref[t])[:shard]
+        lax.fori_loop(0, nz, home, 0)
+
+    rows_done(u_ref, (nplane - 1) * nz, u_recv.at[1])
+    for cb in range(2 * nblk):
+        for zz in range(nz):
+            for yy in range(2):
+                t = (cb * nz + zz) * 2 + yy
+                ucol_ref[t * shard : (t + 1) * shard, :] = column_of(u_ref[(cb * 2 + yy) * nz + zz])[:shard]
+
+    def phase(base, count):
+        row_phase(x_ref, t_ref, ucol_ref, mask_ref, peak_ref, total_ref, base, count, ntb)
+
+    phase(c * ntb + b * per_group, per_group)
+
+    def far(k, _):
+        bb = (b + 1 + k // nz) % nblk
+        @pl.when(c == 0)
+        def _():
+            pass_on(bb, (z + k) % nz, y, None)
+        pass_on(bb, (z + k) % nz, 1 - y, None)
+        return 0
+
+    lax.fori_loop(0, nz * (nblk - 1), far, 0)
+    for k in range(1, nblk):
+        phase(c * ntb + (b + k) % nblk * per_group, per_group)
 
     def other_core(k, _):
-        pltpu.make_async_copy(rows_of(me), rows_of(me), pts_recv.at[2 * k + 1 - c]).wait()
+        arrived((1 - c) * (ndev // 2) + k)
         return 0
 
     lax.fori_loop(0, ndev // 2, other_core, 0)
+    phase((1 - c) * ntb, ntb)
     loads[2].wait()
-    loads[3].wait()
-
-    row_pass(x_ref, t_ref, ucol_ref, mask_ref, logw_ref, pot_ref, g_ref, ntb)
+    row_finish(norm_ref, logw_ref, peak_ref, total_ref, pot_ref, g_ref)
     col_pass(x_ref, t_ref, mask_ref, g_ref, gcol_ref, lse_ref, ntb)
 
-    rec_ref[me] = lse_ref[me // per]
-
-    def send_lse(k, _):
-        t, where = target(k)
-        pltpu.make_async_remote_copy(
-            src_ref=lse_ref.at[t // per], dst_ref=rec_ref.at[me], send_sem=lse_send, recv_sem=lse_recv,
-            device_id=where, device_id_type=pl.DeviceIdType.MESH,
-        ).start()
-        return 0
-
-    lax.fori_loop(1, ndev, send_lse, 0)
+    def span(p):
+        return pl.ds(p * keep, keep)
+
+    for k in range(1, nplane):
+        p, where = plane_peer(k)
+        small(lse_ref.at[span(p // 2)], rec_ref.at[span(plane_me)], lse_send.at[0], lse_recv.at[0], where)
+    rec_ref[span(plane_me)] = lse_ref[span(plane_me // 2)]
+    rows_done(rec_ref, (nplane - 1) * keep, lse_recv.at[0])
+    mid_ref[...] = merged(rec_ref[...].reshape(nplane, keep, 1, LANES))
+    for k in range(1, nz):
+        zz, where = z_peer(k)
+        small(mid_ref.at[zz * 2 // per], last_ref.at[z], lse_send.at[1], lse_recv.at[1], where)
+    last_ref[z] = mid_ref[z * 2 // per]
+
+    def drain(count):
+        def one(_, carry):
+            pltpu.make_async_copy(rows_of(me), rows_of(me), pts_send).wait()
+            return carry
+
+        lax.fori_loop(0, count, one, 0)
+
     @pl.when(c == 0)
     def _():
         drain(nz - 1 + nz + 2 * nz * (nblk - 1) + 2 * nz * nblk)
@@ -308,17 +359,14 @@
     def _():
         drain(nz - 1 + nz * (nblk - 1) + nz * nblk + 2 * nz * nblk)
 
-    pltpu.make_async_copy(others, others, u_send).wait()
-    received = rec_ref.at[pl.ds(0, ndev - 1)]
-    pltpu.make_async_copy(received, received, lse_recv).wait()
-    pltpu.make_async_copy(received, received, lse_send).wait()
-    parts = rec_ref[...]
-    peak = jnp.max(parts, axis=0)
-    total = jnp.sum(jnp.exp2(parts - peak[None]), axis=0)
-    lse = peak + jnp.log2(total)
+    rows_done(u_ref, ndev - 1, u_send)
+    rows_done(rec_ref, (nplane - 1) * keep, lse_send.at[0])
+    rows_done(last_ref, nz - 1, lse_recv.at[1])
+    rows_done(last_ref, nz - 1, lse_send.at[1])
+    lse = merged(last_ref[...])
     mine = lse[:, :shard]
     for k in range(1, per):
-        mine = jnp.where(s % per == k, lse[:, k * shard : (k + 1) * shard], mine)
+        mine = jnp.where((z * 2 + y) % per == k, lse[:, k * shard : (k + 1) * shard], mine)
     next_ref[...] = EPS * (tlogw_ref[...] - mine * LN2 + tnorm * (1.0 / 64.0))
 
 
@@ -330,8 +378,9 @@
     nt = shard * ndev
     ntb = nt // BLOCK
     nrow = pts // LANES
+    keep = nsrc * shard // 2 // LANES
     vmem = pl.BlockSpec(memory_space=pltpu.VMEM)
-    hbm = pl.BlockSpec(memory_space=pl.ANY)
+    hbm = pl.BlockSpec(memory_space=pltpu.HBM)
     f32 = jnp.float32
     pot, fresh = pl.pallas_call(
         functools.partial(fused_kernel, ntb, nsrc, nblk),
@@ -349,17 +398,22 @@
             pltpu.VMEM((pts, LANES), f32),
             pltpu.VMEM((ndev, 1, LANES), f32),
             pltpu.VMEM((nt // LANES, 1, LANES), f32),
-            pltpu.VMEM((ndev, 1, LANES), f32),
+            pltpu.VMEM((4 * nblk * keep, 1, LANES), f32),
+            pltpu.VMEM((keep, 1, LANES), f32),
+            pltpu.VMEM((nsrc // 4, 1, LANES), f32),
+            pltpu.VMEM((nrow, 1, LANES), f32),
+            pltpu.VMEM((nrow, 1, LANES), f32),
+            pltpu.VMEM((nrow, 1, LANES), f32),
             pltpu.SemaphoreType.DMA((4,)),
             pltpu.SemaphoreType.DMA,
             pltpu.SemaphoreType.DMA((ndev,)),
             pltpu.SemaphoreType.DMA,
-            pltpu.SemaphoreType.DMA,
-            pltpu.SemaphoreType.DMA,
-            pltpu.SemaphoreType.DMA,
+            pltpu.SemaphoreType.DMA((2,)),
+            pltpu.SemaphoreType.DMA((2,)),
+            pltpu.SemaphoreType.DMA((2,)),
         ],
         compiler_params=pltpu.CompilerParams(
-            collective_id=0, has_side_effects=True, vmem_limit_bytes=48 * 1024 * 1024
+            collective_id=0, has_side_effects=True, vmem_limit_bytes=63 * 1024 * 1024
         ),
     )(
         source_points,

time: 46.5 us -> 44.9 us (0.966)
  local copies, waits for them, and re-layouts: 5.15 us -> 1.81 us
  Pallas kernels: 40.4 us -> 42.2 us
    unnamed x16 -> x4, local copies, waits for them, and re-layouts: 5.15 us -> 1.81 us
    pallas_call x1, Pallas kernels: 40.4 us -> 42.2 us  [body(): pl.pallas_call(functools.partial(fused_kernel, ntb, nsrc, nblk), out_shap...]
where the time goes in v2:
time: 44.9 us; the launch traced here: 44.7 us
  Pallas kernels  42.2 us (94%)
  local copies, waits for them, and re-layouts  1.81 us (4%)
  between operations  0.65 us (1%)
    pallas_call x1, Pallas kernels, body(): pl.pallas_call(functools.partial(fused_kernel, ntb, nsrc, nblk), out_shap...  42.2 us
    unnamed x4, local copies, waits for them, and re-layouts  1.81 us

profile of v2, /device:TPU:0, one launch (start us, length us, event | category | flops | bytes accessed | tf_op | source)
XLA Modules:
  0.0 44.7 jit_solution(2019138126776662369)
XLA Ops:
  0.6 42.2 %shard_map.86 = (f32[16,1,128]{2,1,0:T(1,128)}, f32[1,64]{1,0:T(1,128)}) custom-call(bf16[2048,256]{1,0:T(8,128)(2,1)} %x_hbm.1, s32[1,2048]{1,0:T(1,128)} %slot_hbm.1, f32[16,1,128]{2,1,0:T(1,128)} %bitcast.5, bf16[64,256]{1,0:T(8,128)(2,1)} %tp_hbm.1, bf16[1,64]{1,0:T(2,128)(2,1)} %bitcast.7, f32[1,64]{1,0:T(1,128)} %bitcast.8, s32[4,4]{1,0:T(4,128)} %pm_ref.1), custom_call_target="tpu_custom_call" | custom-call | tf_op jit(solution)/shard_map/pallas_call | solution.py:385
  42.9 0.0 copy-start
  42.9 1.3 %copy.11 = f32[2048]{0:T(1024)} copy(f32[2048]{0:T(1024)} %bitcast.6) | data formatting | bytes 16384
  44.2 0.0 copy-done
  44.2 0.5 %copy.12 = f32[64]{0:T(128)} copy(f32[64]{0:T(128)S(1)} %bitcast.9) | data formatting | bytes 512
Async XLA Ops:
  42.9 1.3 %copy-start = (f32[1,64]{1,0:T(1,128)S(1)}, f32[1,64]{1,0:T(1,128)}, u32[]{:S(2)}) copy-start(f32[1,64]{1,0:T(1,128)} %get-tuple-element.5) | copy-start | bytes 772

commit v3 on v2

--- a/solution.py
+++ b/solution.py
@@ -96,7 +96,7 @@
             total_ref[2 * ch + h] = total[:, cut]
         return 0
 
-    lax.fori_loop(0, nrow // 2, one_chunk, 0)
+    lax.fori_loop(0, nrow // 2, one_chunk, 0, unroll=2)
 
 
 def row_finish(norm_ref, logw_ref, peak_ref, total_ref, pot_ref, g_ref):
@@ -133,7 +133,7 @@
             out_ref[2 * ch + 1] = lse[:, LANES:]
             return 0
 
-        lax.fori_loop(0, BLOCK // CHUNK, one_chunk, 0)
+        lax.fori_loop(0, BLOCK // CHUNK, one_chunk, 0, unroll=True)
         return 0
 
     lax.fori_loop(0, ntb, one_block, 0)

time: 44.9 us -> 40.1 us (0.89)
  Pallas kernels: 42.2 us -> 37.4 us
    pallas_call x1, Pallas kernels: 42.2 us -> 37.4 us  [body(): pl.pallas_call(functools.partial(fused_kernel, ntb, nsrc, nblk), out_shap...]
where the time goes in v3:
time: 40.1 us; the launch traced here: 39.9 us
  Pallas kernels  37.4 us (93%)
  local copies, waits for them, and re-layouts  1.81 us (5%)
  between operations  0.65 us (2%)
    pallas_call x1, Pallas kernels, body(): pl.pallas_call(functools.partial(fused_kernel, ntb, nsrc, nblk), out_shap...  37.4 us
    unnamed x4, local copies, waits for them, and re-layouts  1.81 us

profile of v3, /device:TPU:0, one launch (start us, length us, event | category | flops | bytes accessed | tf_op | source)
XLA Modules:
  0.0 39.9 jit_solution(15251694431154089402)
XLA Ops:
  0.6 37.4 %shard_map.86 = (f32[16,1,128]{2,1,0:T(1,128)}, f32[1,64]{1,0:T(1,128)}) custom-call(bf16[2048,256]{1,0:T(8,128)(2,1)} %x_hbm.1, s32[1,2048]{1,0:T(1,128)} %slot_hbm.1, f32[16,1,128]{2,1,0:T(1,128)} %bitcast.5, bf16[64,256]{1,0:T(8,128)(2,1)} %tp_hbm.1, bf16[1,64]{1,0:T(2,128)(2,1)} %bitcast.7, f32[1,64]{1,0:T(1,128)} %bitcast.8, s32[4,4]{1,0:T(4,128)} %pm_ref.1), custom_call_target="tpu_custom_call" | custom-call | tf_op jit(solution)/shard_map/pallas_call | solution.py:385
  38.0 0.0 copy-start
  38.0 1.3 %copy.11 = f32[2048]{0:T(1024)} copy(f32[2048]{0:T(1024)} %bitcast.6) | data formatting | bytes 16384
  39.3 0.0 copy-done
  39.3 0.5 %copy.12 = f32[64]{0:T(128)} copy(f32[64]{0:T(128)S(1)} %bitcast.9) | data formatting | bytes 512
Async XLA Ops:
  38.0 1.3 %copy-start = (f32[1,64]{1,0:T(1,128)S(1)}, f32[1,64]{1,0:T(1,128)}, u32[]{:S(2)}) copy-start(f32[1,64]{1,0:T(1,128)} %get-tuple-element.5) | copy-start | bytes 772
